TPU v7x, 32 devices: a whole 2x2x4 slice. The times are simulated.
32 devices in a mesh: fsdp: 8 (over y, x, core), inner: 4 (over z).
Axes of the slice: x: 2, y: 2, z: 4, core: 2. Of those that a mesh axis runs over, the one named last changes fastest.
Arguments:
- tokens: bfloat16 [32768, 1024], P(('fsdp', 'inner')), may hold values from -6 to 6
- doc_starts: int32 [32768], P(('fsdp', 'inner')), may hold values 0 or 1
- w_qkv: bfloat16 [1024, 3072], P('fsdp', 'inner'), may hold values from -0.1875 to 0.1875
- w_dense: bfloat16 [1024, 1024], P('fsdp', 'inner'), may hold values from -0.75 to 0.75
- w_up: bfloat16 [1024, 4096], P('fsdp', 'inner'), may hold values from -0.1875 to 0.1875
- w_down: bfloat16 [4096, 1024], P('fsdp', 'inner'), may hold values from -0.09375 to 0.09375
- norm1_gain: float32 [1024], P('fsdp'), may hold values from 0.5 to 1.5
- norm1_bias: float32 [1024], P('fsdp'), may hold values from -3 to 3
- norm2_gain: float32 [1024], P('fsdp'), may hold values from 0.5 to 1.5
- norm2_bias: float32 [1024], P('fsdp'), may hold values from -3 to 3
- feature_weight: float32 [1024], P('fsdp'), may hold values from 0.25 to 4
- cotangent: bfloat16 [32768, 1024], P(('fsdp', 'inner')), may hold values from -6 to 6
Outputs:
- output: bfloat16 [32768, 1024], P(('fsdp', 'inner'))
- input_grad: float32 [32768, 1024], P(('fsdp', 'inner'))
- grad_qkv: float32 [1024, 3072], P('fsdp', 'inner')
- grad_dense: float32 [1024, 1024], P('fsdp', 'inner')
- grad_up: float32 [1024, 4096], P('fsdp', 'inner')
- grad_down: float32 [4096, 1024], P('fsdp', 'inner')
- grad_gain_one: float32 [1024], P('fsdp')
- grad_bias_one: float32 [1024], P('fsdp')
- grad_gain_two: float32 [1024], P('fsdp')
- grad_bias_two: float32 [1024], P('fsdp')
- grad_feature: float32 [1024], P('fsdp')
All inputs are finite; a program needn't handle non-finite values. No bound on the sum of `doc_starts` on one device may be relied on, other than what follows from the above.
Results may differ from a plain program's by a relative error of at most 0.025.
Values may be sent and summed in bfloat16 or wider, within the bound.
A program may use at most 256 MiB of HBM per device.

v0:
```python
from functools import partial
import math

import jax
import jax.numpy as jnp
from jax import lax
from jax.sharding import PartitionSpec as P

D = 1024
HEADS = 16
HEAD = 64
ROT = 16
FEATS = 64
SEQ_LEN = 1024


PRECISION_BEST = lax.Precision.HIGHEST


def rounded(values):
    lowered = lax.optimization_barrier(values.astype(jnp.bfloat16)).astype(jnp.float32)
    return values + lax.stop_gradient(lowered - values)


def layer_norm(values, gain, bias):
    center = values - jnp.mean(values, axis=-1, keepdims=True)
    spread = jnp.mean(center * center, axis=-1, keepdims=True)
    return center * lax.rsqrt(spread + 1e-05) * gain + bias


def rotary_tables():
    places = jnp.arange(SEQ_LEN, dtype=jnp.float32)
    powers = jnp.arange(0, ROT, 2, dtype=jnp.float32) / ROT
    freqs = 1.0 / 10000.0**powers
    angles = places[:, None] * freqs[None, :]
    cosine_pos = jnp.concatenate([jnp.cos(angles), jnp.cos(angles)], axis=-1)
    sine_pos = jnp.concatenate([jnp.sin(angles), jnp.sin(angles)], axis=-1)
    return (cosine_pos, sine_pos)


def feature_tables():
    order_k = jnp.arange(HEAD, dtype=jnp.int32)[:, None]
    order_i = jnp.arange(HEAD, dtype=jnp.int32)[None, :]
    waves = jnp.cos(
        math.pi * (order_i.astype(jnp.float32) + 0.5) * order_k.astype(jnp.float32) / HEAD
    )
    cosine = jnp.where(order_k == 0, math.sqrt(1.0 / HEAD), math.sqrt(2.0 / HEAD)) * waves
    points = jnp.arange(FEATS, dtype=jnp.int32)[None, :]
    lattice = (points * (2 * order_k + 1) + order_k) % FEATS
    levels = (lattice.astype(jnp.float32) + 0.5) / FEATS
    normals = math.sqrt(2.0) * lax.erf_inv(2.0 * levels - 1.0)
    return jnp.dot(cosine.T, normals, precision=PRECISION_BEST) / math.sqrt(HEAD)


def rotary(heads_in, cosine_pos, sine_pos):
    turning = heads_in[..., :ROT]
    resting = heads_in[..., ROT:]
    middle_split = ROT // 2
    swapped = jnp.concatenate([-turning[..., middle_split:], turning[..., :middle_split]], axis=-1)
    turned = turning * cosine_pos[:, None, :] + swapped * sine_pos[:, None, :]
    return jnp.concatenate([turned, resting], axis=-1)


def attend(query_feat, key_feat, values, doc):
    stride = math.gcd(SEQ_LEN, 512)
    steps_count = SEQ_LEN // stride
    query_steps = query_feat.reshape(steps_count, stride, HEADS * FEATS)
    key_steps = key_feat.reshape(steps_count, stride, HEADS * FEATS)
    value_steps = values.reshape(steps_count, stride, HEADS * HEAD)
    doc_steps = doc.reshape(steps_count, stride)
    causal_mask = jnp.arange(stride)[:, None] >= jnp.arange(stride)[None, :]

    def advance(carry, piece):
        running_key_state, key_total, state_doc = carry
        query_flattened, key_flat, value_flat, doc_part = piece
        query_slice = query_flattened.reshape(stride, HEADS, FEATS)
        key_slice = key_flat.reshape(stride, HEADS, FEATS)
        value_portion = value_flat.reshape(stride, HEADS, HEAD)
        doc_last = doc_part[stride - 1]
        permitted_mask = ((doc_part[:, None] == doc_part[None, :]) & causal_mask).astype(
            jnp.float32
        )
        attention_scores = (
            jnp.einsum("rdj,ydj->dry", query_slice, key_slice, precision=PRECISION_BEST)
            * permitted_mask[None]
        )
        carried = (doc_part == state_doc).astype(jnp.float32)
        numerator = jnp.einsum(
            "hqk,khe->qhe", attention_scores, value_portion, precision=PRECISION_BEST
        )
        numerator = numerator + carried[:, None, None] * jnp.einsum(
            "qhf,hfe->qhe", query_slice, running_key_state, precision=PRECISION_BEST
        )
        denominator = jnp.sum(attention_scores, axis=2).T
        denominator = denominator + carried[:, None] * jnp.einsum(
            "qhf,hf->qh", query_slice, key_total, precision=PRECISION_BEST
        )
        result = (numerator / denominator[:, :, None]).reshape(stride, HEADS * HEAD)
        remains_visible = (state_doc == doc_last).astype(jnp.float32)
        trailing_keys = key_slice * (doc_part == doc_last).astype(jnp.float32)[:, None, None]
        running_key_state = remains_visible * running_key_state + jnp.einsum(
            "bcm,bcn->cmn", trailing_keys, value_portion, precision=PRECISION_BEST
        )
        key_total = remains_visible * key_total + jnp.sum(trailing_keys, axis=0)
        return ((running_key_state, key_total, doc_last), result)

    start_state = (
        jnp.zeros((HEADS, FEATS, HEAD), jnp.float32),
        jnp.zeros((HEADS, FEATS), jnp.float32),
        jnp.array(-1, dtype=jnp.int32),
    )
    unused_state, results = lax.scan(
        jax.checkpoint(advance), start_state, (query_steps, key_steps, value_steps, doc_steps)
    )
    return results.reshape(SEQ_LEN, HEADS * HEAD)


def attention_core(projected, feature_weight, doc, cosine_pos, sine_pos, mixing_matrix):
    rows_here = projected.shape[0]
    seq_count = rows_here // SEQ_LEN
    queries = projected[:, :D].reshape(seq_count, SEQ_LEN, HEADS, HEAD)
    keys_all = projected[:, D : 2 * D].reshape(seq_count, SEQ_LEN, HEADS, HEAD)
    values_all = projected[:, 2 * D :].reshape(seq_count, SEQ_LEN, HEADS * HEAD)
    weights_hf = feature_weight.reshape(HEADS, FEATS)
    query_feat = rounded(
        weights_hf
        * jnp.exp(
            jnp.einsum(
                "slhe,ef->slhf",
                rotary(queries, cosine_pos, sine_pos),
                mixing_matrix,
                precision=PRECISION_BEST,
            )
        )
    )
    key_feat = rounded(
        weights_hf
        * jnp.exp(
            jnp.einsum(
                "slhe,ef->slhf",
                rotary(keys_all, cosine_pos, sine_pos),
                mixing_matrix,
                precision=PRECISION_BEST,
            )
        )
    )
    query_flattened = query_feat.reshape(seq_count, SEQ_LEN, HEADS * FEATS)
    key_flat = key_feat.reshape(seq_count, SEQ_LEN, HEADS * FEATS)
    values_low = rounded(values_all)
    attended = jax.vmap(attend)(query_flattened, key_flat, values_low, doc)
    return attended.reshape(rows_here, D)


def collect(
    w_qkv, w_dense, w_up, w_down, gain_first, bias_first, gain_second, bias_second, feature
):
    widened = (
        lax.all_gather(w_qkv, "inner", axis=1, tiled=True),
        lax.all_gather(w_dense, "inner", axis=1, tiled=True),
        lax.all_gather(w_up, "inner", axis=1, tiled=True),
        lax.all_gather(w_down, "inner", axis=1, tiled=True),
    )
    joined = (
        lax.all_gather(widened[0], "fsdp", axis=0, tiled=True),
        lax.all_gather(widened[1], "fsdp", axis=0, tiled=True),
        lax.all_gather(widened[2], "fsdp", axis=0, tiled=True),
        lax.all_gather(widened[3], "fsdp", axis=0, tiled=True),
        lax.all_gather(gain_first.astype(jnp.bfloat16), "fsdp", axis=0, tiled=True).astype(
            gain_first.dtype
        ),
        lax.all_gather(bias_first.astype(jnp.bfloat16), "fsdp", axis=0, tiled=True).astype(
            bias_first.dtype
        ),
        lax.all_gather(gain_second.astype(jnp.bfloat16), "fsdp", axis=0, tiled=True).astype(
            gain_second.dtype
        ),
        lax.all_gather(bias_second.astype(jnp.bfloat16), "fsdp", axis=0, tiled=True).astype(
            bias_second.dtype
        ),
        lax.all_gather(feature.astype(jnp.bfloat16), "fsdp", axis=0, tiled=True).astype(
            feature.dtype
        ),
    )
    return (joined[:4], joined[4:])


def settle(
    grad_one,
    grad_two,
    grad_three,
    grad_four,
    vector_one,
    vector_two,
    vector_three,
    vector_four,
    vector_five,
):
    summed = lax.psum((vector_one, vector_two, vector_three, vector_four, vector_five), "inner")
    owned = (
        lax.psum_scatter(grad_one, "fsdp", scatter_dimension=0, tiled=True),
        lax.psum_scatter(grad_two, "fsdp", scatter_dimension=0, tiled=True),
        lax.psum_scatter(grad_three, "fsdp", scatter_dimension=0, tiled=True),
        lax.psum_scatter(grad_four, "fsdp", scatter_dimension=0, tiled=True),
        lax.psum_scatter(summed[0], "fsdp", scatter_dimension=0, tiled=True),
        lax.psum_scatter(summed[1], "fsdp", scatter_dimension=0, tiled=True),
        lax.psum_scatter(summed[2], "fsdp", scatter_dimension=0, tiled=True),
        lax.psum_scatter(summed[3], "fsdp", scatter_dimension=0, tiled=True),
        lax.psum_scatter(summed[4], "fsdp", scatter_dimension=0, tiled=True),
    )
    narrowed = (
        lax.psum_scatter(
            owned[0].astype(jnp.bfloat16), "inner", scatter_dimension=1, tiled=True
        ).astype(jnp.float32),
        lax.psum_scatter(
            owned[1].astype(jnp.bfloat16), "inner", scatter_dimension=1, tiled=True
        ).astype(jnp.float32),
        lax.psum_scatter(
            owned[2].astype(jnp.bfloat16), "inner", scatter_dimension=1, tiled=True
        ).astype(jnp.float32),
        lax.psum_scatter(
            owned[3].astype(jnp.bfloat16), "inner", scatter_dimension=1, tiled=True
        ).astype(jnp.float32),
    )
    return (
        narrowed[0],
        narrowed[1],
        narrowed[2],
        narrowed[3],
        owned[4],
        owned[5],
        owned[6],
        owned[7],
        owned[8],
    )


def over_rows(left, right):
    return lax.dot_general(
        left, right, (((0,), (0,)), ((), ())), preferred_element_type=jnp.float32
    )


def by_transpose(left, right):
    return lax.dot_general(
        left, right, (((1,), (1,)), ((), ())), preferred_element_type=jnp.float32
    )


def body(
    tokens,
    doc_starts,
    w_qkv,
    w_dense,
    w_up,
    w_down,
    norm1_gain,
    norm1_bias,
    norm2_gain,
    norm2_bias,
    feature_weight,
    cotangent,
):
    matrices, vectors = collect(
        w_qkv, w_dense, w_up, w_down, norm1_gain, norm1_bias, norm2_gain, norm2_bias, feature_weight
    )
    full_qkv, full_dense, full_up, full_down = matrices
    gain_first, bias_first, gain_second, bias_second, feature_full = vectors
    inputs = tokens.astype(jnp.float32)
    seq_count = tokens.shape[0] // SEQ_LEN
    doc = jnp.cumsum(doc_starts.reshape(seq_count, SEQ_LEN), axis=1)
    cosine_pos, sine_pos = rotary_tables()
    mixing_matrix = feature_tables()
    normed_attn, norm_first_pull = jax.vjp(layer_norm, inputs, gain_first, bias_first)
    normed_mlp, norm_second_pull = jax.vjp(layer_norm, inputs, gain_second, bias_second)
    attn_in = normed_attn.astype(jnp.bfloat16)
    mlp_in = normed_mlp.astype(jnp.bfloat16)
    projected = jnp.dot(attn_in, full_qkv, preferred_element_type=jnp.float32)

    def core(projected_values, feature_values):
        return attention_core(
            projected_values, feature_values, doc, cosine_pos, sine_pos, mixing_matrix
        )

    attended, core_pull = jax.vjp(core, projected, feature_full)
    mixed_low = attended.astype(jnp.bfloat16)
    attn_branch = jnp.dot(mixed_low, full_dense, preferred_element_type=jnp.float32)
    hidden_pre = jnp.dot(mlp_in, full_up, preferred_element_type=jnp.float32)
    hidden_act, gelu_pull = jax.vjp(partial(jax.nn.gelu, approximate=False), hidden_pre)
    hidden_low = hidden_act.astype(jnp.bfloat16)
    mlp_branch = jnp.dot(hidden_low, full_down, preferred_element_type=jnp.float32)
    output = (inputs + attn_branch + mlp_branch).astype(jnp.bfloat16)
    shards = lax.optimization_barrier(
        (
            w_qkv,
            w_dense,
            w_up,
            w_down,
            norm1_gain,
            norm1_bias,
            norm2_gain,
            norm2_bias,
            feature_weight,
            output,
        )
    )
    matrices, unused_vectors = collect(
        shards[0],
        shards[1],
        shards[2],
        shards[3],
        shards[4],
        shards[5],
        shards[6],
        shards[7],
        shards[8],
    )
    full_qkv, full_dense, full_up, full_down = matrices
    grad_down = over_rows(hidden_low, cotangent)
    hidden_grad = by_transpose(cotangent, full_down)
    pre_grad = gelu_pull(hidden_grad)[0].astype(jnp.bfloat16)
    grad_up = over_rows(mlp_in, pre_grad)
    mlp_in_grad = by_transpose(pre_grad, full_up)
    input_second, gain_second_grad, bias_second_grad = norm_second_pull(mlp_in_grad)
    grad_dense = over_rows(mixed_low, cotangent)
    mixed_grad = by_transpose(cotangent, full_dense).astype(jnp.bfloat16).astype(jnp.float32)
    projected_grad, feature_grad = core_pull(mixed_grad)
    projected_low = projected_grad.astype(jnp.bfloat16)
    grad_qkv = over_rows(attn_in, projected_low)
    attn_in_grad = by_transpose(projected_low, full_qkv)
    input_first, gain_first_grad, bias_first_grad = norm_first_pull(attn_in_grad)
    input_grad = cotangent.astype(jnp.float32) + input_first + input_second
    settled = settle(
        grad_qkv,
        grad_dense,
        grad_up,
        grad_down,
        gain_first_grad,
        bias_first_grad,
        gain_second_grad,
        bias_second_grad,
        feature_grad,
    )
    return (
        output,
        input_grad,
        settled[0],
        settled[1],
        settled[2],
        settled[3],
        settled[4],
        settled[5],
        settled[6],
        settled[7],
        settled[8],
    )


def solution(mesh):
    in_specs = (
        P(("fsdp", "inner"), None),
        P(("fsdp", "inner")),
        P("fsdp", "inner"),
        P("fsdp", "inner"),
        P("fsdp", "inner"),
        P("fsdp", "inner"),
        P("fsdp"),
        P("fsdp"),
        P("fsdp"),
        P("fsdp"),
        P("fsdp"),
        P(("fsdp", "inner"), None),
    )
    out_specs = (
        P(("fsdp", "inner"), None),
        P(("fsdp", "inner"), None),
        P("fsdp", "inner"),
        P("fsdp", "inner"),
        P("fsdp", "inner"),
        P("fsdp", "inner"),
        P("fsdp"),
        P("fsdp"),
        P("fsdp"),
        P("fsdp"),
        P("fsdp"),
    )
    return jax.shard_map(body, mesh=mesh, in_specs=in_specs, out_specs=out_specs, check_vma=False)
```

profile of v0, /device:TPU:0, one launch (start us, length us, event | category | flops | bytes accessed | tf_op | source)
XLA Modules:
  0.0 1581.0 jit_solution(7261535672904541129)
XLA Ops:
  8.7 27.1 %all_gather.66 = bf16[128,3072]{1,0:T(8,128)(2,1)} all-gather(bf16[128,768]{1,0:T(8,128)(2,1)} %param.18), channel_id=1, replica_groups=mesh['fsdp'=8,'inner'=4] {'inner'}, dimensions={1}, use_global_device_ids=true | all-gather | bytes 983040 | tf_op jit(solution)/shard_map/all_gather | solution.py:158
  35.9 18.0 %all_gather.68 = bf16[128,1024]{1,0:T(8,128)(2,1)} all-gather(bf16[128,256]{1,0:T(8,128)(2,1)} %param.19), channel_id=1, replica_groups=mesh['fsdp'=8,'inner'=4] {'inner'}, dimensions={1}, use_global_device_ids=true | all-gather | bytes 327680 | tf_op jit(solution)/shard_map/all_gather | solution.py:159
  55.3 8.7 all-gather.4
  65.3 8.7 all-gather.3
  83.6 8.7 all-gather.1
  106.4 20.4 %all-gather.18.cloned.1.call-done = bf16[1024,3072]{1,0:T(8,128)(2,1)} async-done(((bf16[128,3072]{1,0:T(8,128)(2,1)}), bf16[1024,3072]{1,0:T(8,128)(2,1)}) %all-gather.18.cloned.1.call-update) | async-done | bytes 6291472 | tf_op jit(solution)/shard_map/all_gather | solution.py:164
  126.8 9.0 fusion.278
  218.2 111.4 %while.46 = (s32[]{:T(128)}, f32[1,16,64,64]{3,2,1,0:T(8,128)S(1)}, f32[1,16,64]{2,1,0:T(8,128)S(1)}, s32[1]{0:T(128)}, bf16[2,1,512,1024]{3,2,0,1:T(8,128)(2,1)...) while((s32[]{:T(128)}, f32[1,16,64,64]{3,2,1,0:T(8,128)S(1)}, ...), condition=%wide.region_7.8_spmd.clone, body=%wide.region_4.7_spmd.clone.sunk | while | flops 7271690240 | bytes 112988504 | solution.py:112
  239.6 14.8 multiply_reduce_fusion.9
  254.4 13.1 fusion.406
  290.3 14.8 multiply_reduce_fusion.9
  305.1 13.1 fusion.406
  336.4 50.4 %multiply_convert_fusion = (bf16[1024,4096]{1,0:T(8,128)(2,1)}, f32[1024,4096]{1,0:T(8,128)}, f32[1024,4096]{1,0:T(8,128)}) fusion(bf16[1024,4096]{1,0:T(8,128)(2,1)} %all-gather.24.cloned.1.call-done, bf16[1024,1024]{1,0:T(8,128)(2,1)S(1)} %copy-done.24, f32[1024]{0:T(1024)S(1)} %bitcast.592, f32[1024]{0:T(1024)S(1)} %bitcast.580, ...), kind=kOutput, calls=%fused_computation.124 | convolution fusion | flops 8868855808 | bytes 52445184 | tf_op jit(solution)/shard_map/dot_general | solution.py:287
  386.9 15.5 fusion.120
  409.9 16.5 %all_gather.76 = bf16[128,1024]{1,0:T(8,128)(2,1)} all-gather(bf16[128,256]{1,0:T(8,128)(2,1)S(1)} %copy-done.49), channel_id=1, replica_groups=mesh['fsdp'=8,'inner'=4] {'inner'}, dimensions={1}, use_global_device_ids=true | all-gather | bytes 327680 | tf_op jit(solution)/shard_map/all_gather | solution.py:159
  435.6 55.2 %reduce-scatter.13.cloned.1.call-done = f32[128,1024]{1,0:T(8,128)} async-done(((f32[1024,1024]{1,0:T(8,128)}), f32[128,1024]{1,0:T(8,128)}) %reduce-scatter.13.cloned.1.call-update) | async-done | bytes 524304 | tf_op jit(solution)/shard_map/reduce_scatter | solution.py:201
  492.6 28.1 %all-gather.30.cloned.1.call-done = bf16[1024,1024]{1,0:T(8,128)(2,1)} async-done(((bf16[128,1024]{1,0:T(8,128)(2,1)}), bf16[1024,1024]{1,0:T(8,128)(2,1)}) %all-gather.30.cloned.1.call-update) | async-done | bytes 2097168 | tf_op jit(solution)/shard_map/all_gather | solution.py:165
  535.3 454.2 %while.47 = (s32[]{:T(128)}, f32[1,16,64,64]{2,3,1,0:T(8,128)}, f32[1,16,64]{2,1,0:T(8,128)S(1)}, f32[2,1,512,1024]{2,0,3,1:T(2,128)}, f32[2,1,512,1024]{2,0,3,1...) while((s32[]{:T(128)}, f32[1,16,64,64]{2,3,1,0:T(8,128)}, ...), condition=%wide.region_11.12_spmd.clone, body=%wide.region_8.11_spmd.clone.sunk | while | flops 21398007808 | bytes 320904064 | solution.py:112
  562.2 14.7 multiply_reduce_fusion.10
  577.5 14.5 fusion.435
  592.0 18.1 %fusion.441 = f32[16,64,512]{2,1,0:T(8,128)} fusion(f32[16,512,512]{1,2,0:T(8,128)S(1)} %get-tuple-element.921, f32[512,512]{0,1:T(8,128)S(1)} %and_convert_fusion.2, f32[512,16]{0,1:T(8,128)} %get-tuple-element.916, f32[1,512,1024]{1,2,0:T(8,128)} %bitcast.532), kind=kOutput, calls=%fused_computation.43.clone.1 | convolution fusion | flops 3225944064 | bytes 22052864 | tf_op jit(solution)/shard_map/transpose(jvp(vmap()))/while/body/eval_jaxpr/checkpoint/hqk,khe->qhe/dot_general | solution.py:88
  627.2 13.6 fusion.438
  640.8 20.0 %bitcast_add_fusion.6 = f32[1,512,16,64]{1,3,2,0:T(8,128)} fusion(f32[16,64,512]{2,1,0:T(8,128)} %fusion.440, f32[512,16,64]{0,2,1:T(8,128)S(1)} %bitcast.527, f32[16,512,512]{1,2,0:T(8,128)S(1)} %fusion.438, f32[16,512]{1,0:T(8,128)S(1)} %negate_bitcast_fusion.2, f32[512,512]{0,1:T(8,128)S(1)} %and_convert_fusion.2, f32[512]{0:T(512)S(1)} %bitcast.578, ...), kind=kOutput, calls=%fused_computation.54.clone.1 | convolution fusion | flops 3231186944 | bytes 24156160 | tf_op jit(solution)/shard_map/transpose(jvp(vmap()))/while/body/eval_jaxpr/checkpoint/rdj,ydj->dry/dot_general | solution.py:84
  660.8 13.7 fusion.439
  683.0 37.9 %dynamic_update_slice.67 = f32[2,1,512,1024]{2,0,3,1:T(2,128)} dynamic-update-slice(f32[2,1,512,1024]{2,0,3,1:T(2,128)} %get-tuple-element.988, f32[1,1,512,1024]{2,0,3,1:T(1,128)} %copy.178, s32[]{:T(128)S(6)} %sub.126, s32[]{:T(128)} %constant.97.clone.1..sunk.1, s32[]{:T(128)} %constant.97.clone.1..sunk.1, s32[]{:T(128)} %constant.97.clone.1..sunk.1) | dynamic-update-slice | bytes 4194308 | tf_op jit(solution)/shard_map/transpose(jvp(vmap()))/while/body/jit(dynamic_update_index_in_dim)/dynamic_update_slice | solution.py:112
  720.9 37.9 %dynamic_update_slice.66 = f32[2,1,512,1024]{2,0,3,1:T(2,128)} dynamic-update-slice(f32[2,1,512,1024]{2,0,3,1:T(2,128)} %get-tuple-element.987, f32[1,1,512,1024]{2,0,3,1:T(1,128)S(1)} %copy.177, s32[]{:T(128)S(6)} %sub.126, s32[]{:T(128)} %constant.97.clone.1..sunk.1, s32[]{:T(128)} %constant.97.clone.1..sunk.1, s32[]{:T(128)} %constant.97.clone.1..sunk.1) | dynamic-update-slice | bytes 4194308 | tf_op jit(solution)/shard_map/transpose(jvp(vmap()))/while/body/jit(dynamic_update_index_in_dim)/dynamic_update_slice | solution.py:112
  786.5 14.7 multiply_reduce_fusion.10
  801.8 14.3 fusion.435
  816.1 18.1 %fusion.441 = f32[16,64,512]{2,1,0:T(8,128)} fusion(f32[16,512,512]{1,2,0:T(8,128)S(1)} %get-tuple-element.921, f32[512,512]{0,1:T(8,128)S(1)} %and_convert_fusion.2, f32[512,16]{0,1:T(8,128)} %get-tuple-element.916, f32[1,512,1024]{1,2,0:T(8,128)} %bitcast.532), kind=kOutput, calls=%fused_computation.43.clone.1 | convolution fusion | flops 3225944064 | bytes 22052864 | tf_op jit(solution)/shard_map/transpose(jvp(vmap()))/while/body/eval_jaxpr/checkpoint/hqk,khe->qhe/dot_general | solution.py:88
  851.0 13.6 fusion.438
  864.7 20.2 %bitcast_add_fusion.6 = f32[1,512,16,64]{1,3,2,0:T(8,128)} fusion(f32[16,64,512]{2,1,0:T(8,128)} %fusion.440, f32[512,16,64]{0,2,1:T(8,128)S(1)} %bitcast.527, f32[16,512,512]{1,2,0:T(8,128)S(1)} %fusion.438, f32[16,512]{1,0:T(8,128)S(1)} %negate_bitcast_fusion.2, f32[512,512]{0,1:T(8,128)S(1)} %and_convert_fusion.2, f32[512]{0:T(512)S(1)} %bitcast.578, ...), kind=kOutput, calls=%fused_computation.54.clone.1 | convolution fusion | flops 3231186944 | bytes 24156160 | tf_op jit(solution)/shard_map/transpose(jvp(vmap()))/while/body/eval_jaxpr/checkpoint/rdj,ydj->dry/dot_general | solution.py:84
  884.9 13.7 fusion.439
  906.9 37.9 %dynamic_update_slice.67 = f32[2,1,512,1024]{2,0,3,1:T(2,128)} dynamic-update-slice(f32[2,1,512,1024]{2,0,3,1:T(2,128)} %get-tuple-element.988, f32[1,1,512,1024]{2,0,3,1:T(1,128)} %copy.178, s32[]{:T(128)S(6)} %sub.126, s32[]{:T(128)} %constant.97.clone.1..sunk.1, s32[]{:T(128)} %constant.97.clone.1..sunk.1, s32[]{:T(128)} %constant.97.clone.1..sunk.1) | dynamic-update-slice | bytes 4194308 | tf_op jit(solution)/shard_map/transpose(jvp(vmap()))/while/body/jit(dynamic_update_index_in_dim)/dynamic_update_slice | solution.py:112
  944.8 37.9 %dynamic_update_slice.66 = f32[2,1,512,1024]{2,0,3,1:T(2,128)} dynamic-update-slice(f32[2,1,512,1024]{2,0,3,1:T(2,128)} %get-tuple-element.987, f32[1,1,512,1024]{2,0,3,1:T(1,128)S(1)} %copy.177, s32[]{:T(128)S(6)} %sub.126, s32[]{:T(128)} %constant.97.clone.1..sunk.1, s32[]{:T(128)} %constant.97.clone.1..sunk.1, s32[]{:T(128)} %constant.97.clone.1..sunk.1) | dynamic-update-slice | bytes 4194308 | tf_op jit(solution)/shard_map/transpose(jvp(vmap()))/while/body/jit(dynamic_update_index_in_dim)/dynamic_update_slice | solution.py:112
  1038.8 16.2 %fusion.271 = f32[1024,3072]{1,0:T(8,128)} fusion(f32[1024,1024]{1,0:T(8,128)} %copy.107, f32[1024,1024]{1,0:T(8,128)} %copy.105, f32[1024,1024]{1,0:T(8,128)} %bitcast.560, bf16[1024,1024]{1,0:T(8,128)(2,1)S(1)} %copy-done.25, f32[1024]{0:T(1024)S(1)} %bitcast.595, f32[1024]{0:T(1024)S(1)} %bitcast.586, f32[1024]{0:T(1024)S(1)} %copy-done.64, ...), kind=kOutput, calls=%fused_computation.363 | convolution fusion | flops 6458179584 | bytes 27279360 | tf_op jit(solution)/shard_map/dot_general | solution.py:238
  1055.6 17.9 %fusion.294 = f32[4096,1024]{1,0:T(8,128)} fusion(bf16[1024,4096]{1,0:T(8,128)(2,1)} %get-tuple-element.657, bf16[1024,1024]{1,0:T(8,128)(2,1)} %param.27), kind=kOutput, calls=%fused_computation.381 | convolution fusion | flops 8589934592 | bytes 27262976 | tf_op jit(solution)/shard_map/dot_general | solution.py:238
  1074.5 19.8 %all_gather.78 = bf16[128,3072]{1,0:T(8,128)(2,1)} all-gather(bf16[128,768]{1,0:T(8,128)(2,1)S(1)} %copy-done.40), channel_id=1, replica_groups=mesh['fsdp'=8,'inner'=4] {'inner'}, dimensions={1}, use_global_device_ids=true | all-gather | bytes 983040 | tf_op jit(solution)/shard_map/all_gather | solution.py:158
  1094.4 26.7 %fusion.93 = bf16[1024,4096]{1,0:T(8,128)(2,1)} fusion(f32[1024,4096]{1,0:T(8,128)} %get-tuple-element.658, f32[1024,4096]{1,0:T(8,128)} %get-tuple-element.698, bf16[4096,1024]{1,0:T(8,128)(2,1)} %all-gather.36.cloned.1.call-done, bf16[1024,1024]{1,0:T(8,128)(2,1)} %param.27), kind=kOutput, calls=%fused_computation.122 | convolution fusion | flops 8648654848 | bytes 52428800 | tf_op jit(solution)/shard_map/dot_general | solution.py:244
  1121.0 15.2 fusion.273
  1149.7 53.7 %all-gather.40.cloned.1.call-done = bf16[1024,4096]{1,0:T(8,128)(2,1)} async-done(((bf16[128,4096]{1,0:T(8,128)(2,1)}), bf16[1024,4096]{1,0:T(8,128)(2,1)}) %all-gather.40.cloned.1.call-update) | async-done | bytes 8388624 | tf_op jit(solution)/shard_map/all_gather | solution.py:166
  1203.4 15.3 fusion.292
  1218.6 104.2 %reduce-scatter.21.cloned.1.call-done = f32[512,1024]{1,0:T(8,128)} async-done(((f32[4096,1024]{1,0:T(8,128)}), f32[512,1024]{1,0:T(8,128)}) %reduce-scatter.21.cloned.1.call-update) | async-done | bytes 2097168 | tf_op jit(solution)/shard_map/reduce_scatter | solution.py:203
  1325.6 44.4 %all-gather.32.cloned.1.call-done = bf16[1024,3072]{1,0:T(8,128)(2,1)} async-done(((bf16[128,3072]{1,0:T(8,128)(2,1)}), bf16[1024,3072]{1,0:T(8,128)(2,1)}) %all-gather.32.cloned.1.call-update) | async-done | bytes 6291472 | tf_op jit(solution)/shard_map/all_gather | solution.py:164
  1370.1 14.2 fusion.283
  1384.3 105.2 %reduce-scatter.17.cloned.1.call-done = f32[128,4096]{1,0:T(8,128)} async-done(((f32[1024,4096]{1,0:T(8,128)}), f32[128,4096]{1,0:T(8,128)}) %reduce-scatter.17.cloned.1.call-update) | async-done | bytes 2097168 | tf_op jit(solution)/shard_map/reduce_scatter | solution.py:202
  1497.7 24.1 %all-reduce.16 = (f32[1024]{0:T(1024)S(1)}, f32[1024]{0:T(1024)S(1)}, f32[1024]{0:T(1024)S(1)}, f32[1024]{0:T(1024)S(1)}, f32[1024]{0:T(1024)S(1)}) all-reduce(f32[1024]{0:T(1024)S(1)} %get-tuple-element.588, f32[1024]{0:T(1024)S(1)} %get-tuple-element.585, ...), channel_id=10, replica_groups=mesh['fsdp'=8,'inner'=4] {'fsdp'}, use_global_device_ids=true, to_apply=%region_26.27.clone | all-reduce | flops 5120 | bytes 40960
  1522.2 12.4 all-reduce.17
  1545.6 26.3 %reduce-scatter.19.cloned.1.call-done = bf16[128,1024]{1,0:T(8,128)(2,1)} async-done(((bf16[128,4096]{1,0:T(8,128)(2,1)}), bf16[128,1024]{1,0:T(8,128)(2,1)}) %reduce-scatter.19.cloned.1.call-update) | async-done | bytes 262160 | tf_op jit(solution)/shard_map/reduce_scatter | solution.py:217
  (437 shorter events, 383.7 us)
Async XLA Ops:
  7.2 98.1 %copy-start.23 = (bf16[1024,1024]{1,0:T(8,128)(2,1)S(1)}, bf16[1024,1024]{1,0:T(8,128)(2,1)}, u32[]{:S(2)}) copy-start(bf16[1024,1024]{1,0:T(8,128)(2,1)} %param.16) | copy-start | bytes 6291460
  7.2 46.8 %all-gather.22.cloned.1.call-start = ((), (), s32[]{:S(2)}) async-start(), calls=%async_computation.10 | async-start | bytes 1310720 | tf_op jit(solution)/shard_map/all_gather | solution.py:160
  7.9 98.4 %all-gather.26.cloned.1.call-start = ((), (), s32[]{:S(2)}) async-start(), calls=%async_computation.12 | async-start | bytes 1310720 | tf_op jit(solution)/shard_map/all_gather | solution.py:161
  8.7 118.1 %all-gather.18.cloned.1.call-start = ((), (), s32[]{:S(2)}) async-start(), calls=%async_computation.8 | async-start | bytes 7077888 | tf_op jit(solution)/shard_map/all_gather | solution.py:164
  35.9 293.7 %all-gather.20.cloned.1.call-start = ((), (), s32[]{:S(2)}) async-start(), calls=%async_computation.9 | async-start | bytes 2359296 | tf_op jit(solution)/shard_map/all_gather | solution.py:165
  53.9 282.5 %all-gather.24.cloned.1.call-start = ((), (), s32[]{:S(2)}) async-start(), calls=%async_computation.11 | async-start | bytes 9437184 | tf_op jit(solution)/shard_map/all_gather | solution.py:166
  54.5 332.3 %all-gather.28.cloned.1.call-start = ((), (), s32[]{:S(2)}) async-start(), calls=%async_computation.13 | async-start | bytes 9437184 | tf_op jit(solution)/shard_map/all_gather | solution.py:167
  83.0 52.8 %copy-start.67 = (f32[8,1,128]{2,1,0:T(1,128)}, f32[8,1,128]{2,1,0:T(1,128)S(1)}, u32[]{:S(2)}) copy-start(f32[8,1,128]{2,1,0:T(1,128)S(1)} %convert_element_type.238) | copy-start | bytes 12292
  92.4 43.4 %copy-start.60 = (f32[8,1,128]{2,1,0:T(1,128)}, f32[8,1,128]{2,1,0:T(1,128)S(1)}, u32[]{:S(2)}) copy-start(f32[8,1,128]{2,1,0:T(1,128)S(1)} %convert_element_type.237) | copy-start | bytes 12292
  100.9 88.1 %copy-start.51 = (f32[16,64]{1,0:T(8,128)}, f32[16,64]{1,0:T(8,128)S(1)}, u32[]{:S(2)}) copy-start(f32[16,64]{1,0:T(8,128)S(1)} %reshape.956) | copy-start | bytes 12292
  103.1 70.8 %copy-start.41 = (f32[1024,16]{0,1:T(8,128)}, f32[1024,16]{0,1:T(8,128)S(1)}, u32[]{:S(2)}) copy-start(f32[1024,16]{0,1:T(8,128)S(1)} %get-tuple-element.704) | copy-start | bytes 196612
  103.2 70.8 %copy-start.43 = (f32[1024,16]{0,1:T(8,128)}, f32[1024,16]{0,1:T(8,128)S(1)}, u32[]{:S(2)}) copy-start(f32[1024,16]{0,1:T(8,128)S(1)} %get-tuple-element.705) | copy-start | bytes 196612
  103.6 78.5 %copy-start.45 = (f32[64,64,1]{1,0,2:T(8,128)}, f32[64,64,1]{1,0,2:T(8,128)S(1)}, u32[]{:S(2)}) copy-start(f32[64,64,1]{1,0,2:T(8,128)S(1)} %fusion.146) | copy-start | bytes 49156
  105.6 30.2 %copy-start.53 = (f32[1024]{0:T(1024)}, f32[1024]{0:T(1024)S(1)}, u32[]{:S(2)}) copy-start(f32[1024]{0:T(1024)S(1)} %broadcast_multiply_fusion) | copy-start | bytes 12292
  106.3 29.5 %copy-start.56 = (f32[1024]{0:T(1024)}, f32[1024]{0:T(1024)S(1)}, u32[]{:S(2)}) copy-start(f32[1024]{0:T(1024)S(1)} %fusion.116) | copy-start | bytes 12292
  106.3 29.5 %copy-start.62 = (f32[1024]{0:T(1024)}, f32[1024]{0:T(1024)S(1)}, u32[]{:S(2)}) copy-start(f32[1024]{0:T(1024)S(1)} %fusion.237) | copy-start | bytes 12292
  106.4 329.1 %all-gather.34.cloned.1.call-start = ((), (), s32[]{:S(2)}) async-start(), calls=%async_computation.16 | async-start | bytes 1310720 | tf_op jit(solution)/shard_map/all_gather | solution.py:161
  402.4 88.4 %reduce-scatter.13.cloned.1.call-start = ((), (), s32[]{:S(2)}) async-start(), calls=%async_computation.22 | async-start | bytes 4718592 | tf_op jit(solution)/shard_map/reduce_scatter | solution.py:201
  409.1 111.7 %copy-start.37 = (bf16[1024,1024]{1,0:T(8,128)(2,1)S(1)}, bf16[1024,1024]{1,0:T(8,128)(2,1)}, u32[]{:S(2)}) copy-start(bf16[1024,1024]{1,0:T(8,128)(2,1)} %param.27) | copy-start | bytes 6291460
  409.1 111.6 %all-gather.30.cloned.1.call-start = ((), (), s32[]{:S(2)}) async-start(), calls=%async_computation.14 | async-start | bytes 2359296 | tf_op jit(solution)/shard_map/all_gather | solution.py:165
  426.5 628.6 %all-gather.38.cloned.1.call-start = ((), (), s32[]{:S(2)}) async-start(), calls=%async_computation.18 | async-start | bytes 1310720 | tf_op jit(solution)/shard_map/all_gather | solution.py:160
  427.1 667.3 %all-gather.36.cloned.1.call-start = ((), (), s32[]{:S(2)}) async-start(), calls=%async_computation.17 | async-start | bytes 9437184 | tf_op jit(solution)/shard_map/all_gather | solution.py:167
  435.5 702.6 %reduce-scatter.15.cloned.1.call-start = ((), (), s32[]{:S(2)}) async-start(), calls=%async_computation.23 | async-start | bytes 327680 | tf_op jit(solution)/shard_map/reduce_scatter | solution.py:214
  492.6 654.6 %reduce-scatter.9.cloned.1.call-start = ((), (), s32[]{:S(2)}) async-start(), calls=%async_computation.20 | async-start | bytes 14155776 | tf_op jit(solution)/shard_map/reduce_scatter | solution.py:200
  538.3 15.9 %copy-start.38 = (f32[1,16,64]{2,1,0:T(8,128)}, f32[1,16,64]{2,1,0:T(8,128)S(1)}, u32[]{:S(2)}) copy-start(f32[1,16,64]{2,1,0:T(8,128)S(1)} %dynamic-slice_bitcast_fusion.10) | copy-start | bytes 12292 | tf_op jit(solution)/shard_map/transpose(jvp(vmap()))/while
  547.5 14.7 copy-start
  550.3 26.5 %copy-start.7 = (f32[1,512,1024]{1,2,0:T(8,128)}, f32[1,512,1024]{1,2,0:T(8,128)S(1)}, u32[]{:S(2)}) copy-start(f32[1,512,1024]{1,2,0:T(8,128)S(1)} %get-tuple-element.914) | copy-start | bytes 6291460 | tf_op jit(solution)/shard_map/transpose(jvp(vmap()))/while
  592.0 18.1 %copy-start.8 = (f32[1,512,1024]{1,2,0:T(8,128)S(1)}, f32[1,512,1024]{1,2,0:T(8,128)}, u32[]{:S(2)}) copy-start(f32[1,512,1024]{1,2,0:T(8,128)} %copy-done.7) | copy-start | bytes 6291460 | tf_op jit(solution)/shard_map/transpose(jvp(vmap()))/while
  592.0 18.1 %copy-start.16 = (f32[1,16,64,64]{2,3,1,0:T(8,128)S(1)}, f32[1,16,64,64]{2,3,1,0:T(8,128)}, u32[]{:S(2)}) copy-start(f32[1,16,64,64]{2,3,1,0:T(8,128)} %broadcast_select_fusion.6) | copy-start | bytes 786436 | tf_op jit(solution)/shard_map/transpose(jvp(vmap()))/while
  592.0 18.1 %copy-start.47 = (f32[1,512]{1,0:T(1,128)S(1)}, f32[1,512]{1,0:T(1,128)}, u32[]{:S(2)}) copy-start(f32[1,512]{1,0:T(1,128)} %get-tuple-element.925) | copy-start | bytes 6148 | tf_op jit(solution)/shard_map/transpose(jvp(vmap()))/while
  683.0 75.8 %copy-start.50 = (f32[1,16,64]{2,1,0:T(8,128)S(1)}, f32[1,16,64]{2,1,0:T(8,128)}, u32[]{:S(2)}) copy-start(f32[1,16,64]{2,1,0:T(8,128)} %bitcast_add_fusion.5) | copy-start | bytes 12292 | tf_op jit(solution)/shard_map/transpose(jvp(vmap()))/while
  761.6 16.9 %copy-start.38 = (f32[1,16,64]{2,1,0:T(8,128)}, f32[1,16,64]{2,1,0:T(8,128)S(1)}, u32[]{:S(2)}) copy-start(f32[1,16,64]{2,1,0:T(8,128)S(1)} %dynamic-slice_bitcast_fusion.10) | copy-start | bytes 12292 | tf_op jit(solution)/shard_map/transpose(jvp(vmap()))/while
  771.8 14.7 copy-start
  774.6 26.6 %copy-start.7 = (f32[1,512,1024]{1,2,0:T(8,128)}, f32[1,512,1024]{1,2,0:T(8,128)S(1)}, u32[]{:S(2)}) copy-start(f32[1,512,1024]{1,2,0:T(8,128)S(1)} %get-tuple-element.914) | copy-start | bytes 6291460 | tf_op jit(solution)/shard_map/transpose(jvp(vmap()))/while
  816.1 18.1 %copy-start.8 = (f32[1,512,1024]{1,2,0:T(8,128)S(1)}, f32[1,512,1024]{1,2,0:T(8,128)}, u32[]{:S(2)}) copy-start(f32[1,512,1024]{1,2,0:T(8,128)} %copy-done.7) | copy-start | bytes 6291460 | tf_op jit(solution)/shard_map/transpose(jvp(vmap()))/while
  816.1 18.1 %copy-start.16 = (f32[1,16,64,64]{2,3,1,0:T(8,128)S(1)}, f32[1,16,64,64]{2,3,1,0:T(8,128)}, u32[]{:S(2)}) copy-start(f32[1,16,64,64]{2,3,1,0:T(8,128)} %broadcast_select_fusion.6) | copy-start | bytes 786436 | tf_op jit(solution)/shard_map/transpose(jvp(vmap()))/while
  816.1 18.1 %copy-start.47 = (f32[1,512]{1,0:T(1,128)S(1)}, f32[1,512]{1,0:T(1,128)}, u32[]{:S(2)}) copy-start(f32[1,512]{1,0:T(1,128)} %get-tuple-element.925) | copy-start | bytes 6148 | tf_op jit(solution)/shard_map/transpose(jvp(vmap()))/while
  906.9 75.8 %copy-start.50 = (f32[1,16,64]{2,1,0:T(8,128)S(1)}, f32[1,16,64]{2,1,0:T(8,128)}, u32[]{:S(2)}) copy-start(f32[1,16,64]{2,1,0:T(8,128)} %bitcast_add_fusion.5) | copy-start | bytes 12292 | tf_op jit(solution)/shard_map/transpose(jvp(vmap()))/while
  1055.0 148.3 %all-gather.40.cloned.1.call-start = ((), (), s32[]{:S(2)}) async-start(), calls=%async_computation.19 | async-start | bytes 9437184 | tf_op jit(solution)/shard_map/all_gather | solution.py:166
  1055.6 267.2 %reduce-scatter.21.cloned.1.call-start = ((), (), s32[]{:S(2)}) async-start(), calls=%async_computation.26 | async-start | bytes 18874368 | tf_op jit(solution)/shard_map/reduce_scatter | solution.py:203
  1073.6 296.5 %all-gather.32.cloned.1.call-start = ((), (), s32[]{:S(2)}) async-start(), calls=%async_computation.15 | async-start | bytes 7077888 | tf_op jit(solution)/shard_map/all_gather | solution.py:164
  1094.3 395.2 %reduce-scatter.17.cloned.1.call-start = ((), (), s32[]{:S(2)}) async-start(), calls=%async_computation.24 | async-start | bytes 18874368 | tf_op jit(solution)/shard_map/reduce_scatter | solution.py:202
  1094.3 26.7 %copy-start.59 = (f32[8,1,128]{2,1,0:T(1,128)S(1)}, f32[8,1,128]{2,1,0:T(1,128)}, u32[]{:S(2)}) copy-start(f32[8,1,128]{2,1,0:T(1,128)} %convert_element_type.239) | copy-start | bytes 12292
  1094.3 26.7 %copy-start.66 = (f32[8,1,128]{2,1,0:T(1,128)S(1)}, f32[8,1,128]{2,1,0:T(1,128)}, u32[]{:S(2)}) copy-start(f32[8,1,128]{2,1,0:T(1,128)} %convert_element_type.240) | copy-start | bytes 12292
  1136.3 405.1 %reduce-scatter.11.cloned.1.call-start = ((), (), s32[]{:S(2)}) async-start(), calls=%async_computation.21 | async-start | bytes 983040 | tf_op jit(solution)/shard_map/reduce_scatter | solution.py:211
  1149.6 394.2 %reduce-scatter.23.cloned.1.call-start = ((), (), s32[]{:S(2)}) async-start(), calls=%async_computation.27 | async-start | bytes 1310720 | tf_op jit(solution)/shard_map/reduce_scatter | solution.py:220
  1325.6 58.7 %copy-start.57 = (f32[1024]{0:T(1024)S(1)}, f32[1024]{0:T(1024)}, u32[]{:S(2)}) copy-start(f32[1024]{0:T(1024)} %copy-done.56) | copy-start | bytes 12292
  1325.6 246.3 %reduce-scatter.19.cloned.1.call-start = ((), (), s32[]{:S(2)}) async-start(), calls=%async_computation.25 | async-start | bytes 1310720 | tf_op jit(solution)/shard_map/reduce_scatter | solution.py:217
  (69 other events, 433.7 us)
Sparse Core Ops, SparseCore 0:
  9.6 39.6 all-gather.21
  50.9 30.0 all-gather.25
  82.9 43.8 all-gather.17
  128.5 27.8 all-gather.19
  158.2 54.3 all-gather.23
  214.4 54.3 all-gather.27
  402.5 32.8 all-gather.33
  439.4 51.3 reduce-scatter.12
  492.8 27.8 all-gather.29
  522.2 27.9 all-gather.37
  552.3 53.8 all-gather.35
  609.0 19.5 reduce-scatter.14
  1055.1 92.0 reduce-scatter.8
  1148.9 54.3 all-gather.39
  1206.8 115.9 reduce-scatter.20
  1324.5 45.4 all-gather.31
  1373.5 115.9 reduce-scatter.16
  1491.6 23.2 reduce-scatter.10
  1517.2 26.5 reduce-scatter.22
  1546.1 25.7 reduce-scatter.18
where the time goes:
time: 1600 us; the launch traced here: 1580 us
  matrix products  525 us (33%)
  waiting for transfers between devices  451 us (28%)
  local copies, waits for them, and re-layouts  317 us (20%)
  blocking collectives  160 us (10%)
  other arithmetic  89 us (6%)
  loops' own time  23.1 us (1%)
  between operations  16.2 us (1%)
    dynamic_update_slice x18, local copies, waits for them, and re-layouts, attend(): lax.scan(jax.checkpoint(advance), start_state, (query_steps, key_steps, v...  181 us
    dot_general x8, matrix products, advance(): jnp.einsum('rdj,ydj->dry', query_slice, key_slice, precision=PRECISION_BEST)  126 us
    dot_general x8, matrix products, advance(): jnp.einsum('hqk,khe->qhe', attention_scores, value_portion, precision=PRE...  118 us
    reduce_scatter x1, waiting for transfers between devices, settle(): lax.psum_scatter(grad_three, 'fsdp', scatter_dimension=0, tiled=True)  105 us
    reduce_scatter x1, waiting for transfers between devices, settle(): lax.psum_scatter(grad_four, 'fsdp', scatter_dimension=0, tiled=True)  104 us
    all_gather x2, waiting for transfers between devices, collect(): lax.all_gather(widened[0], 'fsdp', axis=0, tiled=True)  64.8 us
    dot_general x4, matrix products, by_transpose(): lax.dot_general(left, right, (((1,), (1,)), ((), ())), preferred_element_...  62.1 us
    dot_general x4, matrix products, over_rows(): lax.dot_general(left, right, (((0,), (0,)), ((), ())), preferred_element_...  55.9 us
  transfers between devices with their start and end apart: 20, of which 11 were waited for; matrix products, arithmetic and copies ran while one was open for 57% of the time, Pallas kernels for 0%

commit v1 on v0

v1 whole, which is shorter than its diff:
```python
from functools import partial
import math
from statistics import NormalDist

import jax
import jax.numpy as jnp
import numpy as np
from jax import lax
from jax.experimental import pallas as pl
from jax.experimental.pallas import tpu as pltpu
from jax.sharding import PartitionSpec as P

MESH = pl.DeviceIdType.MESH
BF16 = jnp.bfloat16
F32 = jnp.float32


HEAD = 64
ROT = 16
FEATS = 64
SEQ_LEN = 1024

class Place:
    def __init__(self, nf, nz):
        self.nf, self.nz = nf, nz
        self.nbits = (nf // 2).bit_length() - 1
        self.f = lax.axis_index("fsdp")
        self.z = lax.axis_index("inner")
        self.core = lax.rem(self.f, 2)
        self.bits = [lax.rem(lax.div(self.f, 2 << b), 2) for b in range(self.nbits)]

    def partner(self):
        return (self.f + 1 - 2 * self.core, self.z)

    def across(self, b):
        return (self.f + (1 - 2 * self.bits[b]) * (2 << b), self.z)

    def along(self, step):
        return (self.f, self.z + step)

    def slot(self, done, flip=None):
        index = []
        for b in reversed(range(self.nbits)):
            if b in done:
                index.append(slice(None))
            elif b == flip:
                index.append(1 - self.bits[b])
            else:
                index.append(self.bits[b])
        return tuple(index)

    def columns(self, buf, zsel):
        if zsel is None:
            return slice(None)
        width = buf.shape[-1] // self.nz
        return pl.ds(pl.multiple_of(zsel * width, width), width)

    def greet(self, far=False):
        bar = pltpu.get_barrier_semaphore()
        z, nz = self.z, self.nz
        fixed = [self.partner()] + [self.across(b) for b in range(self.nbits)]
        for peer in fixed:
            pl.semaphore_signal(bar, inc=1, device_id=peer, device_id_type=MESH)

        @pl.when(z > 0)
        def _():
            pl.semaphore_signal(bar, inc=1, device_id=self.along(-1), device_id_type=MESH)

        @pl.when(z < nz - 1)
        def _():
            pl.semaphore_signal(bar, inc=1, device_id=self.along(1), device_id_type=MESH)

        count = len(fixed)
        if far and nz > 2:
            step = 2
            while step < nz:
                pl.semaphore_signal(
                    bar, inc=1, device_id=self.fold(step), device_id_type=MESH
                )
                count += 1
                step *= 2
        inner = (z > 0).astype(jnp.int32) + (z < nz - 1).astype(jnp.int32)
        pl.semaphore_wait(bar, count + inner)

    def fold(self, step):
        bit = lax.rem(lax.div(self.z, step), 2)
        return (self.f, self.z + (1 - 2 * bit) * step)


class Sems:
    def __init__(self, send, recv):
        self.send, self.recv, self.count = send, recv, 0

    def take(self):
        self.count += 1
        return self.count - 1

    def copy(self, src, dst, i, peer):
        return pltpu.make_async_remote_copy(
            src_ref=src,
            dst_ref=dst,
            send_sem=self.send.at[i],
            recv_sem=self.recv.at[i],
            device_id=peer,
            device_id_type=MESH,
        )


def shares(rows):
    units = rows // 16
    last = units // 4
    first = (units - last + 1) // 2
    sizes = [first * 16, (units - last - first) * 16, last * 16]
    starts = [0, sizes[0], sizes[0] + sizes[1]]
    return list(zip(starts, sizes))


def orders(nbits):
    up, down = list(range(nbits)), list(reversed(range(nbits)))
    return [["z"] + up, ["z"] + down, up + ["z"]]


def copies_of(nz, nbits):
    return nbits + 2 * (nz - 1)


def gather_stream(at, sems, buf, start, size, order):
    rows = pl.ds(start, size)
    rounds = []
    done, zdone = (), False

    def along(k, done):
        ids = (sems.take(), sems.take())

        def right(zsel):
            ref = buf.at[at.slot(done) + (rows, at.columns(buf, zsel))]
            return sems.copy(ref, ref, ids[0], at.along(1))

        def left(zsel):
            ref = buf.at[at.slot(done) + (rows, at.columns(buf, zsel))]
            return sems.copy(ref, ref, ids[1], at.along(-1))

        z, nz = at.z, at.nz
        goes_right = (z < nz - 1) & (z - k + 1 >= 0)
        goes_left = (z > 0) & (z + k - 1 <= nz - 1)

        def send():
            pl.when(goes_right)(lambda: right(z - k + 1).start())
            pl.when(goes_left)(lambda: left(z + k - 1).start())

        def arrive():
            pl.when(z - k >= 0)(lambda: right(z - k).wait_recv())
            pl.when(z + k <= nz - 1)(lambda: left(z + k).wait_recv())

        def leave():
            pl.when(goes_right)(lambda: right(z - k + 1).wait_send())
            pl.when(goes_left)(lambda: left(z + k - 1).wait_send())

        return send, arrive, leave

    def across(b, done, zsel):
        i = sems.take()
        mine = buf.at[at.slot(done) + (rows, at.columns(buf, zsel))]
        theirs = buf.at[at.slot(done, flip=b) + (rows, at.columns(buf, zsel))]
        out = sems.copy(mine, mine, i, at.across(b))
        back = sems.copy(theirs, theirs, i, at.across(b))
        return out.start, back.wait_recv, out.wait_send

    for dim in order:
        if dim == "z":
            rounds += [along(k, done) for k in range(1, at.nz)]
            zdone = True
        else:
            rounds.append(across(dim, done, None if zdone else at.z))
            done = done + (dim,)
    return rounds


def scatter_stream(at, sems, acc, holds, start, size, order):
    rows = pl.ds(start, size)
    rounds = []
    left_bits, zleft = set(range(at.nbits)), True

    def along(k, remaining, hold):
        ids = (sems.take(), sems.take())
        z, nz = at.z, at.nz

        def part(zsel):
            return acc.at[at.slot(remaining) + (rows, at.columns(acc, zsel))]

        def right(zsel):
            return sems.copy(part(zsel), hold.at[2 * k - 2], ids[0], at.along(1))

        def left(zsel):
            return sems.copy(part(zsel), hold.at[2 * k - 1], ids[1], at.along(-1))

        goes_right = z + k <= nz - 1
        goes_left = z - k >= 0

        def send():
            pl.when(goes_right)(lambda: right(z + k).start())
            pl.when(goes_left)(lambda: left(z - k).start())

        def arrive():
            @pl.when((z >= 1) & (z - 1 + k <= nz - 1))
            def _():
                right(z - 1 + k).wait_recv()
                ref = part(z - 1 + k)
                ref[...] += hold[2 * k - 2]

            @pl.when((z <= nz - 2) & (z + 1 - k >= 0))
            def _():
                left(z + 1 - k).wait_recv()
                ref = part(z + 1 - k)
                ref[...] += hold[2 * k - 1]

        def leave():
            pl.when(goes_right)(lambda: right(z + k).wait_send())
            pl.when(goes_left)(lambda: left(z - k).wait_send())

        return send, arrive, leave

    def across(b, remaining, zsel, hold):
        i = sems.take()
        out = sems.copy(
            acc.at[at.slot(remaining, flip=b) + (rows, at.columns(acc, zsel))], hold, i, at.across(b)
        )

        def arrive():
            out.wait_recv()
            ref = acc.at[at.slot(remaining) + (rows, at.columns(acc, zsel))]
            ref[...] += hold[...]

        return out.start, arrive, out.wait_send

    holds = iter(holds)
    for dim in reversed(order):
        if dim == "z":
            hold = next(holds)
            rounds += [along(k, tuple(left_bits), hold) for k in range(at.nz - 1, 0, -1)]
            zleft = False
        else:
            left_bits = left_bits - {dim}
            rounds.append(across(dim, tuple(left_bits), None if zleft else at.z, next(holds)))
    return rounds


def hold_shapes(nz, nbits, size, width, order):
    shapes, bits, zleft = [], nbits, True
    for dim in reversed(order):
        if dim == "z":
            shapes.append((2 * (nz - 1),) + (2,) * bits + (size, width // nz))
            zleft = False
        else:
            bits -= 1
            shapes.append((2,) * bits + (size, width if zleft else width // nz))
    return shapes


def gather_kernel(nf, nz, tok, cot, doc, vec, wq, wd, wu, ww,
                  tok2, cot2, doc2, vecs, bq, bd, bu, bw, send, recv, local):
    at = Place(nf, nz)
    sems = Sems(send, recv)
    c, o = at.core, 1 - at.core
    me = at.slot(())
    col = lambda b: at.columns(b, at.z)
    at.greet()
    nlocal = [0]

    def put(src, dst):
        cp = pltpu.make_async_copy(src, dst, local.at[nlocal[0]])
        nlocal[0] += 1
        cp.start()
        return cp

    def swap(src, dst, arrives):
        i = sems.take()
        cp = sems.copy(src, dst, i, at.partner())
        cp.start()
        return cp, sems.copy(src, arrives, i, at.partner())

    rq, ru = wq.shape[1], wu.shape[1]
    mine = lambda r: pl.ds(pl.multiple_of(c * r, r), r)
    other = lambda r: pl.ds(pl.multiple_of(o * r, r), r)
    pairs = [
        swap(wq.at[o], bq.at[me + (mine(rq), col(bq))], bq.at[me + (other(rq), col(bq))]),
        swap(wu.at[o], bu.at[me + (mine(ru), col(bu))], bu.at[me + (other(ru), col(bu))]),
        swap(vec, vecs.at[me + (c,)], vecs.at[me + (o,)]),
        swap(doc, doc2.at[c], doc2.at[o]),
        swap(tok, tok2.at[c], tok2.at[o]),
        swap(cot, cot2.at[c], cot2.at[o]),
    ]
    locals_ = [
        put(wq.at[c], bq.at[me + (mine(rq), col(bq))]),
        put(wd, bd.at[me + (slice(None), col(bd))]),
        put(wu.at[c], bu.at[me + (mine(ru), col(bu))]),
        put(ww, bw.at[me + (slice(None), col(bw))]),
        put(vec, vecs.at[me + (c,)]),
        put(doc, doc2.at[c]),
        put(tok, tok2.at[c]),
        put(cot, cot2.at[c]),
    ]
    streams = []
    for buf in (bq, bd, bu, bw):
        for (start, size), order in zip(shares(buf.shape[-2]), orders(at.nbits)):
            if size:
                streams.append(gather_stream(at, sems, buf, start, size, order))
    small = []
    done = []
    for b in range(at.nbits):
        i = sems.take()
        m = vecs.at[at.slot(done)]
        t = vecs.at[at.slot(done, flip=b)]
        small.append((sems.copy(m, m, i, at.across(b)), sems.copy(t, t, i, at.across(b))))
        done = done + [b]
    for k in range(4):
        locals_[k].wait()
    pairs[0][1].wait_recv()
    pairs[1][1].wait_recv()
    for s in streams:
        s[0][0]()
    locals_[4].wait()
    pairs[2][1].wait_recv()
    for out, back in small:
        out.start()
        back.wait_recv()
    n = len(streams[0])
    for r in range(n):
        for s in streams:
            s[r][1]()
            if r + 1 < n:
                s[r + 1][0]()
    for k in range(5, 8):
        locals_[k].wait()
    for k in range(3, 6):
        pairs[k][1].wait_recv()
    for out, back in pairs:
        out.wait_send()
    for out, back in small:
        out.wait_send()
    for s in streams:
        for r in s:
            r[2]()

def gather(nf, nz, tok, cot, doc, vec, wq, wd, wu, ww):
    bits = (2,) * ((nf // 2).bit_length() - 1)
    nb = len(bits)
    sd = jax.ShapeDtypeStruct
    outs = [
        sd((2,) + tok.shape, BF16), sd((2,) + cot.shape, BF16), sd((2,) + doc.shape, doc.dtype),
        sd(bits + (2,) + vec.shape, F32),
        sd(bits + (2 * wq.shape[1], nz * wq.shape[2]), BF16),
        sd(bits + (wd.shape[0], nz * wd.shape[1]), BF16),
        sd(bits + (2 * wu.shape[1], nz * wu.shape[2]), BF16),
        sd(bits + (ww.shape[0], nz * ww.shape[1]), BF16),
    ]
    n = 6 + nb + 12 * copies_of(nz, nb)
    return pl.pallas_call(
        partial(gather_kernel, nf, nz), out_shape=outs,
        in_specs=[pl.BlockSpec(memory_space=pl.ANY)] * 8,
        out_specs=[pl.BlockSpec(memory_space=pl.ANY)] * 8,
        scratch_shapes=[pltpu.SemaphoreType.DMA((n,)), pltpu.SemaphoreType.DMA((n,)), pltpu.SemaphoreType.DMA((8,))],
        compiler_params=pltpu.CompilerParams(collective_id=0, has_side_effects=True),
        name="gather",
    )(tok, cot, doc, vec, wq, wd, wu, ww)


CH = 256

def dot(a, b):
    return jnp.dot(a, b, preferred_element_type=F32)

def dot_nt(a, b):
    return lax.dot_general(a, b, (((1,), (1,)), ((), ())), preferred_element_type=F32)

def dot_tn(a, b):
    return lax.dot_general(a, b, (((0,), (0,)), ((), ())), preferred_element_type=F32)

def tile(i, n):
    return pl.ds(pl.multiple_of(i * n, n), n)

def loop(n, body):
    lax.fori_loop(0, n, lambda i, _: (body(i), 0)[1], 0)

def lanes(width):
    return lax.broadcasted_iota(jnp.int32, (1, width), 1)

def normed(x):
    center = x - jnp.mean(x, axis=-1, keepdims=True)
    spread = jnp.mean(center * center, axis=-1, keepdims=True)
    rstd = lax.rsqrt(spread + 1e-05)
    return center * rstd, rstd

def attention_kernel(head, rot, tok, cot, vec, fw, wq, wd, mask, carr, trail, keep, cosp, sina, sinb, mixh, mixl, mixt,
                     mlp_in, o, pg, gq, gd, gf, dy1,
                     attn_in, qf, kf, vv, dd, do, st, cur):
    T = tok.shape[0]
    width = qf.shape[1]
    npair = width // 128
    seq = cosp.shape[0]
    nch = T // CH
    half = rot // 2

    def ln(i):
        r = tile(i, CH)
        n, _ = normed(tok[r, :].astype(F32))
        attn_in[r, :] = (n * vec[0:1, :] + vec[1:2, :]).astype(BF16)
        mlp_in[r, :] = (n * vec[2:3, :] + vec[3:4, :]).astype(BF16)
    loop(nch, ln)

    RT = 512
    def project(i):
        r = tile(i, RT)
        p = tile(lax.rem(i, seq // RT), RT)
        a = attn_in[r, :]
        for part, dst in ((0, qf), (1, kf)):
            x = dot(a, wq[:, part * width:(part + 1) * width])
            for m in range(npair):
                s = slice(m * 128, (m + 1) * 128)
                y = x[:, s]
                y = y * cosp[p, :] + pltpu.roll(y, half, 1) * sina[p, :] + pltpu.roll(y, 128 - half, 1) * sinb[p, :]
                hi = y.astype(BF16)
                lo = (y - hi.astype(F32)).astype(BF16)
                e = dot(hi, mixh[...]) + dot(lo, mixh[...]) + dot(hi, mixl[...])
                dst[r, s] = (fw[:, s] * jnp.exp(e)).astype(BF16)
        vv[r, :] = dot(a, wq[:, 2 * width:3 * width]).astype(BF16)
        do[r, :] = dot_nt(cot[r, :], wd[...]).astype(BF16)
    loop(T // RT, project)

    h0 = (lanes(128) % (2 * head)) < head
    h0w = jnp.concatenate([h0, h0], axis=1)
    rowh = (lax.broadcasted_iota(jnp.int32, (128, 1), 0)) < head
    block = rowh == h0w
    same = (rowh == h0).astype(BF16)
    one = jnp.ones((CH, 128), BF16)
    zero = jnp.zeros((), BF16)

    def scores(q, k, v, m):
        s0 = dot_nt(jnp.where(h0, q, zero), k)
        s1 = dot_nt(jnp.where(h0, zero, q), k)
        return (s0 * m).astype(BF16), (s1 * m).astype(BF16)

    cur[...] = jnp.zeros_like(cur)
    place = lanes(128) % head

    def split(x):
        hi = x.astype(BF16)
        return hi, (x - hi.astype(F32)).astype(BF16)

    def forward(i):
        r = tile(i, CH)
        m = mask[r, :].astype(F32)
        cw = jnp.concatenate([carr[r, :], carr[r, :]], axis=1)
        tr = trail[r, :]
        kp = keep[i]
        kpw = jnp.concatenate([kp, kp], axis=1)
        for j in range(npair):
            s = slice(j * 128, (j + 1) * 128)
            q, k, v = qf[r, s], kf[r, s], vv[r, s]
            va = jnp.concatenate([v, one], axis=1)
            p0, p1 = scores(q, k, v, m)
            state = cur[j]
            hi, lo = split(state)
            st[i, j, 0] = hi
            st[i, j, 1] = lo
            res = dot(p0, jnp.where(h0w, va, zero)) + dot(p1, jnp.where(h0w, zero, va)) + cw * (dot(q, hi) + dot(q, lo))
            rd = 1.0 / res[:, 128:]
            att = res[:, :128] * rd
            o[r, s] = att.astype(BF16)
            dnb = (do[r, s].astype(F32) * rd).astype(BF16)
            do[r, s] = dnb
            hi, lo = split(dnb.astype(F32) * att)
            hi, lo = split(-(dot(hi, same) + dot(lo, same)))
            dd[r, s] = jnp.where(place == 0, hi, jnp.where(place == 1, lo, zero))
            kt = (k.astype(F32) * tr).astype(BF16)
            cur[j] = kpw * state + jnp.where(block, dot_tn(kt, va), 0.0)
    loop(nch, forward)

    cur[...] = jnp.zeros_like(cur)
    gf[...] = jnp.zeros_like(gf)

    def backward(ii):
        i = nch - 1 - ii
        r = tile(i, CH)
        p = tile(lax.rem(i, seq // CH), CH)
        m = mask[r, :].astype(F32)
        cr, tr = carr[r, :], trail[r, :]
        kp = keep[i]
        kpw = jnp.concatenate([kp, kp], axis=1)
        cos, sa, sb = cosp[p, :], sina[p, :], sinb[p, :]

        def unfeature(d, f, s, base):
            de = d * f.astype(F32)
            gf[:, s] += jnp.sum(de.reshape(CH // 8, 8, 128), axis=0)
            g = dot(de.astype(BF16), mixt[...])
            g = g * cos + pltpu.roll(g * sa, 128 - half, 1) + pltpu.roll(g * sb, half, 1)
            pg[r, base + s.start:base + s.stop] = g.astype(BF16)

        for j in range(npair):
            s = slice(j * 128, (j + 1) * 128)
            q, k, v = qf[r, s], kf[r, s], vv[r, s]
            va = jnp.concatenate([v, one], axis=1)
            p0, p1 = scores(q, k, v, m)
            dnb = do[r, s]
            dy = jnp.concatenate([dnb, dd[r, s]], axis=1)
            ds0 = (dot_nt(dy, jnp.where(h0w, va, zero)) * m).astype(BF16)
            ds1 = (dot_nt(dy, jnp.where(h0w, zero, va)) * m).astype(BF16)
            dst = cur[j]
            dhi, dlo = split(dst)
            dq = dot(ds0, jnp.where(h0, k, zero)) + dot(ds1, jnp.where(h0, zero, k)) + cr * (dot_nt(dy, st[i, j, 0]) + dot_nt(dy, st[i, j, 1]))
            dk = dot_tn(ds0, jnp.where(h0, q, zero)) + dot_tn(ds1, jnp.where(h0, zero, q)) + tr * (dot_nt(va, dhi) + dot_nt(va, dlo))
            dv = dot_tn(p0, jnp.where(h0, dnb, zero)) + dot_tn(p1, jnp.where(h0, zero, dnb)) + tr * dot(k, dhi[:, :128])
            qc = (q.astype(F32) * cr).astype(BF16)
            cur[j] = kpw * dst + jnp.where(block, dot_tn(qc, dy), 0.0)
            unfeature(dq, q, s, 0)
            unfeature(dk, k, s, width)
            pg[r, 2 * width + s.start:2 * width + s.stop] = dv.astype(BF16)
    loop(nch, backward)

    D = tok.shape[1]
    gd[...] = dot_tn(o[...], cot[...]).astype(BF16)
    def gqkv(i):
        gq[:, tile(i, width)] = dot_tn(attn_in[...], pg[:, tile(i, width)]).astype(BF16)
    loop(3, gqkv)
    def dattn(i):
        r = tile(i, RT)
        dy1[r, :] = dot_nt(pg[r, :], wq[...]).astype(BF16)
    loop(T // RT, dattn)

def attention(head, rot, tok, cot, vec, fw, wq, wd, mask, carr, trail, keep, cosp, sina, sinb, mixh, mixl, mixt):
    T, D = tok.shape
    W = fw.shape[1]
    sd = jax.ShapeDtypeStruct
    vm = pl.BlockSpec(memory_space=pltpu.VMEM)
    outs = [sd((T, D), BF16), sd((T, W), BF16), sd((T, 3 * W), BF16), sd((D, 3 * W), BF16), sd((W, D), BF16), sd((8, W), F32), sd((T, D), BF16)]
    return pl.pallas_call(
        partial(attention_kernel, head, rot), out_shape=outs, in_specs=[vm] * 16, out_specs=[vm] * 7,
        scratch_shapes=[pltpu.VMEM((T, D), BF16), pltpu.VMEM((T, W), BF16), pltpu.VMEM((T, W), BF16), pltpu.VMEM((T, W), BF16),
                        pltpu.VMEM((T, W), BF16), pltpu.VMEM((T, W), BF16), pltpu.VMEM((T // CH, W // 128, 2, 128, 256), BF16), pltpu.VMEM((W // 128, 128, 256), F32)],
        compiler_params=pltpu.CompilerParams(vmem_limit_bytes=62 << 20), name="attention",
    )(tok, cot, vec, fw, wq, wd, mask, carr, trail, keep, cosp, sina, sinb, mixh, mixl, mixt)

def gelu_pair(x):
    e = jnp.exp(-0.5 * x * x)
    t = 1.0 / (1.0 + (0.3275911 / math.sqrt(2.0)) * jnp.abs(x))
    poly = t * (0.254829592 + t * (-0.284496736 + t * (1.421413741 + t * (-1.453152027 + t * 1.061405429))))
    tail = 0.5 * poly * e
    phi = jnp.where(x >= 0, 1.0 - tail, tail)
    return x * phi, phi + x * e * (1.0 / math.sqrt(2.0 * math.pi))

def mlp_kernel(mlp_in, cot, o, wd, wu, ww, out, gu, gw, dy2, h, pre):
    T, D = mlp_in.shape
    FB = 512
    nb = wu.shape[1] // FB
    RT = 512
    def hidden(i):
        m = lax.div(i, T // RT)
        r = tile(lax.rem(i, T // RT), RT)
        c = tile(m, FB)
        hid = dot(mlp_in[r, :], wu[:, c])
        act, slope = gelu_pair(hid)
        h[r, c] = act.astype(BF16)
        pre[r, c] = (dot_nt(cot[r, :], ww[c, :]) * slope).astype(BF16)
    loop(nb * (T // RT), hidden)
    def grads(m):
        c = tile(m, FB)
        gw[c, :] = dot_tn(h[:, c], cot[...]).astype(BF16)
        gu[:, c] = dot_tn(mlp_in[...], pre[:, c]).astype(BF16)
    loop(nb, grads)
    def last(i):
        r = tile(i, RT)
        out[r, :] = (dot(h[r, :], ww[...]) + dot(o[r, :], wd[...])).astype(BF16)
        dy2[r, :] = dot_nt(pre[r, :], wu[...]).astype(BF16)
    loop(T // RT, last)

def mlp(mlp_in, cot, o, wd, wu, ww):
    T, D = mlp_in.shape
    FH = wu.shape[1]
    sd = jax.ShapeDtypeStruct
    vm = pl.BlockSpec(memory_space=pltpu.VMEM)
    outs = [sd((T, D), BF16), sd((D, FH), BF16), sd((FH, D), BF16), sd((T, D), BF16)]
    return pl.pallas_call(mlp_kernel, out_shape=outs, in_specs=[vm] * 6, out_specs=[vm] * 4,
        scratch_shapes=[pltpu.VMEM((T, FH), BF16), pltpu.VMEM((T, FH), BF16)],
        compiler_params=pltpu.CompilerParams(vmem_limit_bytes=62 << 20), name="mlp")(mlp_in, cot, o, wd, wu, ww)

def tables(seq, rot, head, feats):
    half = rot // 2
    angles = np.arange(seq)[:, None] / 10000.0 ** (np.arange(0, rot, 2) / rot)[None, :]
    cosp, sina, sinb = np.ones((seq, 128)), np.zeros((seq, 128)), np.zeros((seq, 128))
    for base in range(0, 128, head):
        cosp[:, base:base + half] = np.cos(angles)
        cosp[:, base + half:base + rot] = np.cos(angles)
        sina[:, base + half:base + rot] = np.sin(angles)
        sinb[:, base:base + half] = -np.sin(angles)
    k, i = np.arange(head)[:, None], np.arange(head)[None, :]
    cosine = np.where(k == 0, math.sqrt(1.0 / head), math.sqrt(2.0 / head)) * np.cos(math.pi * (i + 0.5) * k / head)
    j = np.arange(feats)[None, :]
    level = (((j * (2 * k + 1) + k) % feats) + 0.5) / feats
    normals = np.vectorize(NormalDist().inv_cdf)(level)
    mixing = cosine.T @ normals / math.sqrt(head)
    mix = np.zeros((128, 128), np.float32)
    for base in range(0, 128, head):
        mix[base:base + head, base:base + feats] = mixing
    return cosp.astype(np.float32), sina.astype(np.float32), sinb.astype(np.float32), mix

def doc_masks(doc, seq):
    n = doc.shape[0]
    d = doc.reshape(n, seq // CH, CH)
    causal = jnp.arange(CH)[:, None] >= jnp.arange(CH)[None, :]
    mask = ((d[:, :, :, None] == d[:, :, None, :]) & causal).astype(BF16).reshape(-1, CH)
    last = d[:, :, -1]
    before = jnp.concatenate([jnp.full((n, 1), -1, doc.dtype), last[:, :-1]], axis=1)
    carr = jnp.broadcast_to((d == before[:, :, None]).astype(F32).reshape(-1, 1), (n * seq, 128))
    trail = jnp.broadcast_to((d == last[:, :, None]).astype(F32).reshape(-1, 1), (n * seq, 128))
    keep = jnp.broadcast_to((last == before).astype(F32).reshape(-1, 1, 1), (n * seq // CH, 1, 128))
    return mask, carr, trail, keep


def all_streams(at, sems, accs, holds):
    streams = []
    it = iter(holds)
    nb = at.nbits
    for acc in accs:
        for (start, size), order in zip(shares(acc.shape[-2]), orders(nb)):
            if size:
                n = len(hold_shapes(at.nz, nb, size, acc.shape[-1], order))
                streams.append(scatter_stream(at, sems, acc, [next(it) for _ in range(n)], start, size, order))
    return streams

def settle_kernel(nf, nz, nh, *refs):
    (gq, gd, gu, gw, gf, fw, part, dy1, dy2, tok, cot, vec,
     oq, od, ou, ow, ovec, output, input_grad) = refs[:19]
    aq, ad, au, aw = refs[19:23]
    holds = refs[23:23 + nh]
    hq, hu, pr, gv, vh, send, recv, local = refs[23 + nh:]
    at = Place(nf, nz)
    sems = Sems(send, recv)
    c, o = at.core, 1 - at.core
    rows, D = tok.shape
    at.greet(far=True)
    swaps = []
    for k, ref in enumerate((part, dy1, dy2)):
        cp = sems.copy(ref.at[o], pr.at[2 * k], sems.take(), at.partner())
        cp.start()
        swaps.append(cp)
    loads = []
    for k, (src, dst) in enumerate(((gq, aq), (gd, ad), (gu, au), (gw, aw), (part.at[c], pr.at[1]), (dy1.at[c], pr.at[3]), (dy2.at[c], pr.at[5]))):
        cp = pltpu.make_async_copy(src, dst, local.at[k])
        cp.start()
        loads.append(cp)
    streams = all_streams(at, sems, (aq, ad, au, aw), holds)
    for cp in loads[:4]:
        cp.wait()
    for s in streams:
        s[0][0]()
    for cp in loads[4:]:
        cp.wait()
    for cp in swaps:
        cp.wait_recv()
    gv[...] = jnp.zeros_like(gv)

    def finish(i):
        r = tile(i, CH)
        x = tok[r, :].astype(F32)
        n, rstd = normed(x)
        get = lambda k: pr[2 * k, r, :].astype(F32) + pr[2 * k + 1, r, :].astype(F32)
        output[r, :] = (x + get(0)).astype(BF16)
        d1, d2 = get(1), get(2)
        fold = lambda y: jnp.sum(y, axis=0, keepdims=True)
        gv[0:1, :] += fold(d1 * n)
        gv[1:2, :] += fold(d1)
        gv[2:3, :] += fold(d2 * n)
        gv[3:4, :] += fold(d2)
        dn = d1 * vec[0:1, :] + d2 * vec[2:3, :]
        dx = rstd * (dn - jnp.mean(dn, axis=-1, keepdims=True) - n * jnp.mean(dn * n, axis=-1, keepdims=True))
        input_grad[r, :] = cot[r, :].astype(F32) + dx
    loop(rows // CH, finish)
    for m in range(gf.shape[1] // 128):
        s = slice(m * 128, (m + 1) * 128)
        gv[4:5, pl.ds(pl.multiple_of((2 * m + c) * 128, 128), 128)] = jnp.sum(gf[:, s], axis=0, keepdims=True) / fw[:, s]

    n = len(streams[0])
    for r in range(n):
        for s in streams:
            s[r][1]()
            if r + 1 < n:
                s[r + 1][0]()
    peers = [at.partner()] + [at.across(b) for b in range(at.nbits)]
    step = 1
    while step < nz:
        peers.append(at.fold(step))
        step *= 2
    small = []
    for k, peer in enumerate(peers):
        cp = sems.copy(gv, vh.at[k], sems.take(), peer)
        cp.start()
        cp.wait()
        gv[...] += vh[k]
    ovec[...] = gv[...]
    me = at.slot(())
    last = []
    for acc, hold, out in ((aq, hq, oq), (au, hu, ou)):
        half = hold.shape[0]
        cols = at.columns(acc, at.z)
        cp = sems.copy(acc.at[me + (tile(o, half), cols)], hold, sems.take(), at.partner())
        cp.start()
        out[c] = acc[me + (tile(c, half), cols)]
        last.append((cp, hold, out))
    od[...] = ad[me + (slice(None), at.columns(ad, at.z))]
    ow[...] = aw[me + (slice(None), at.columns(aw, at.z))]
    for cp, hold, out in last:
        cp.wait_recv()
        out[o] = hold[...]
        cp.wait_send()
    for cp in swaps:
        cp.wait_send()
    for s in streams:
        for r in s:
            r[2]()

def settle(nf, nz, gq, gd, gu, gw, gf, fw, part, dy1, dy2, tok, cot, vec):
    sd = jax.ShapeDtypeStruct
    bits = (2,) * ((nf // 2).bit_length() - 1)
    nb, chips = len(bits), nf // 2
    cut = lambda g: g.reshape(bits + (g.shape[0] // chips, g.shape[1]))
    accs = [cut(g) for g in (gq, gd, gu, gw)]
    rows, D = tok.shape
    two = lambda x: x.reshape(2, rows, D)
    own = lambda a: (a.shape[-2], a.shape[-1] // nz)
    holds = []
    for a in accs:
        for (start, size), order in zip(shares(a.shape[-2]), orders(nb)):
            if size:
                holds += hold_shapes(nz, nb, size, a.shape[-1], order)
    halves = [(own(a)[0] // 2, own(a)[1]) for a in (accs[0], accs[2])]
    nsteps = 1 + nb + max(nz.bit_length() - 1, 0)
    ncopies = 3 + 12 * copies_of(nz, nb) + nsteps + 2
    vm, hb = pl.BlockSpec(memory_space=pltpu.VMEM), pl.BlockSpec(memory_space=pl.ANY)
    outs = [sd((2,) + halves[0], BF16), sd(own(accs[1]), BF16), sd((2,) + halves[1], BF16), sd(own(accs[3]), BF16), sd(vec.shape, F32), sd((rows, D), BF16), sd((rows, D), F32)]
    return pl.pallas_call(
        partial(settle_kernel, nf, nz, len(holds)), out_shape=outs,
        in_specs=[hb] * 4 + [vm] * 2 + [hb] * 3 + [vm] * 3, out_specs=[vm] * 7,
        scratch_shapes=[pltpu.VMEM(a.shape, BF16) for a in accs] + [pltpu.VMEM(h, BF16) for h in holds]
        + [pltpu.VMEM(h, BF16) for h in halves] + [pltpu.VMEM((6, rows, D), BF16), pltpu.VMEM(vec.shape, F32), pltpu.VMEM((nsteps,) + vec.shape, F32)]
        + [pltpu.SemaphoreType.DMA((ncopies,)), pltpu.SemaphoreType.DMA((ncopies,)), pltpu.SemaphoreType.DMA((7,))],
        compiler_params=pltpu.CompilerParams(collective_id=1, has_side_effects=True, vmem_limit_bytes=62 << 20), name="settle",
    )(*accs, gf, fw, two(part), two(dy1), two(dy2), tok, cot, vec)

def body(nf, nz, tokens, doc_starts, w_qkv, w_dense, w_up, w_down, norm1_gain, norm1_bias, norm2_gain, norm2_bias, feature_weight, cotangent):
    rows, D = tokens.shape
    core = lax.rem(lax.axis_index("fsdp"), 2)
    width = D // 2
    unit = w_down.shape[0]
    def turn(w, block):
        r, n = w.shape
        return w.reshape(r, n // (2 * block), 2, block).transpose(2, 0, 1, 3).reshape(2, r, n // 2)

    def unturn(g, block):
        two, r, n = g.shape
        return g.reshape(2, r, n // block, block).transpose(1, 2, 0, 3).reshape(r, 2 * n)

    sub = 128 // (2 * w_dense.shape[0])
    pairs = [(f, f ^ 1) for f in range(nf)]

    def heads_of(w):
        if not sub:
            return w
        w = w.reshape(-1, 2, sub, w_dense.shape[0], D)
        kept = lax.dynamic_index_in_dim(w, core, 1, keepdims=False)
        other = lax.ppermute(lax.dynamic_index_in_dim(w, 1 - core, 1, keepdims=False), "fsdp", pairs)
        both = jnp.where(core == 0, jnp.stack([kept, other], 2), jnp.stack([other, kept], 2))
        return both.reshape(-1, D)

    def shards_of(g):
        if not sub:
            return g
        g = g.reshape(-1, sub, 2, w_dense.shape[0], D)
        kept = lax.dynamic_index_in_dim(g, core, 2, keepdims=False)
        other = lax.ppermute(lax.dynamic_index_in_dim(g, 1 - core, 2, keepdims=False), "fsdp", pairs)
        both = jnp.where(core == 0, jnp.stack([kept, other], 1), jnp.stack([other, kept], 1))
        return both.reshape(-1, D)

    doc = jnp.cumsum(doc_starts.reshape(-1, SEQ_LEN), axis=1).astype(jnp.int32)
    vec = jnp.stack([norm1_gain, norm1_bias, norm2_gain, norm2_bias, feature_weight] + [jnp.zeros_like(norm1_gain)] * 3)
    tok2, cot2, doc2, vecs, bq, bd, bu, bw = gather(
        nf, nz, tokens, cotangent, doc.reshape(8, -1), vec, turn(w_qkv, 128), w_dense, turn(w_up, unit), w_down
    )
    join = lambda b: b.reshape(-1, b.shape[-1])
    dense = heads_of(join(bd))
    vec8 = vecs.reshape(nf, 8, -1).transpose(1, 0, 2).reshape(8, D)
    fw = lax.dynamic_index_in_dim(vec8[4].reshape(D // 256, 2, 128), core, 1, keepdims=False).reshape(1, width)
    masks = doc_masks(doc2.reshape(-1, SEQ_LEN), SEQ_LEN)
    cosp, sina, sinb, mix = tables(SEQ_LEN, ROT, HEAD, FEATS)
    mix = jnp.asarray(mix)
    mixh = mix.astype(BF16)
    mixl = (mix - mixh.astype(F32)).astype(BF16)
    tok_all, cot_all = tok2.reshape(2 * rows, D), cot2.reshape(2 * rows, D)
    mlp_in, mixed, pg, gq, gd, gf, dy1 = attention(
        HEAD, ROT, tok_all, cot_all, vec8, fw, join(bq), dense, *masks, cosp, sina, sinb, mixh, mixl, mixh.T
    )
    part, gu, gw, dy2 = mlp(mlp_in, cot_all, mixed, dense, join(bu), join(bw))
    oq, od, ou, ow, gv, output, input_grad = settle(nf, nz, gq, shards_of(gd), gu, gw, gf, fw, part, dy1, dy2, tokens, cotangent, vec8)
    own = gv.reshape(8, nf, -1)
    own = lax.dynamic_index_in_dim(own, lax.axis_index("fsdp"), 1, keepdims=False)
    return (
        output, input_grad,
        unturn(oq, 128).astype(F32), od.astype(F32), unturn(ou, unit).astype(F32), ow.astype(F32),
        own[0], own[1], own[2], own[3], own[4],
    )


def solution(mesh):
    nf, nz = mesh.shape["fsdp"], mesh.shape["inner"]
    rows, mat, vec = P(("fsdp", "inner"), None), P("fsdp", "inner"), P("fsdp")
    in_specs = (rows, P(("fsdp", "inner"))) + (mat,) * 4 + (vec,) * 5 + (rows,)
    out_specs = (rows, rows) + (mat,) * 4 + (vec,) * 5
    return jax.shard_map(partial(body, nf, nz), mesh=mesh, in_specs=in_specs, out_specs=out_specs, check_vma=False)
```

time: 1600 us -> 484 us (0.30); the launches traced: 1580 us -> 483 us
  matrix products: 525 us -> 0 us
  Pallas kernels: 0 us -> 454 us
  waiting for transfers between devices: 451 us -> 0 us
  local copies, waits for them, and re-layouts: 317 us -> 20.2 us
  blocking collectives: 160 us -> 0 us
  other arithmetic: 89 us -> 7.94 us
  loops' own time: 23.1 us -> 0 us
    dot_general x53 -> x0, matrix products: 525 us -> none  [the longest x8 126 us: advance(): jnp.einsum('rdj,ydj->dry', query_slice, key_slice, precision=PRECISION_BEST)]
    pallas_call x0 -> x4, Pallas kernels: none -> 454 us  [the longest x1 150 us: gather(): pl.pallas_call(partial(gather_kernel, nf, nz), out_shape=outs, in_specs=[...]
    reduce_scatter x8 -> x0, waiting for transfers between devices: 292 us -> none  [the longest x1 105 us: settle(): lax.psum_scatter(grad_three, 'fsdp', scatter_dimension=0, tiled=True)]
    dynamic_update_slice x18 -> x0, local copies, waits for them, and re-layouts: 181 us -> none  [attend(): lax.scan(jax.checkpoint(advance), start_state, (query_steps, key_steps, v...]
    all_gather x12 -> x0, waiting for transfers between devices: 155 us -> none  [the longest x2 64.8 us: collect(): lax.all_gather(widened[0], 'fsdp', axis=0, tiled=True)]
    all_gather x9 -> x0, blocking collectives: 123 us -> none  [the longest x2 46.9 us: collect(): lax.all_gather(w_qkv, 'inner', axis=1, tiled=True)]
    unnamed x1 -> x0, blocking collectives: 24.1 us -> none
    another operation x2 -> x0, loops' own time: 23.1 us -> none  [attend(): lax.scan(jax.checkpoint(advance), start_state, (query_steps, key_steps, v...]
  transfers between devices with their start and end apart: 20 -> 0, of which waited for: 11 -> 0; matrix products, arithmetic and copies ran while one was open for 57% -> 0% of each run, Pallas kernels for 0% -> 0%
where the time goes in v1:
time: 484 us; the launch traced here: 483 us
  Pallas kernels  454 us (94%)
  local copies, waits for them, and re-layouts  20.2 us (4%)
  other arithmetic  7.94 us (2%)
    pallas_call x1, Pallas kernels, gather(): pl.pallas_call(partial(gather_kernel, nf, nz), out_shape=outs, in_specs=[...  150 us
    pallas_call x1, Pallas kernels, settle(): pl.pallas_call(partial(settle_kernel, nf, nz, len(holds)), out_shape=outs...  143 us
    pallas_call x1, Pallas kernels, attention(): pl.pallas_call(partial(attention_kernel, head, rot), out_shape=outs, in_s...  87.7 us
    pallas_call x1, Pallas kernels, mlp(): pl.pallas_call(mlp_kernel, out_shape=outs, in_specs=[vm] * 6, out_specs=[...  73.4 us

profile of v1, /device:TPU:0, one launch (start us, length us, event | category | flops | bytes accessed | tf_op | source)
XLA Modules:
  0.0 483.1 jit_solution(15097623181822107374)
XLA Ops:
  0.7 1.3 stack.27.vec
  2.0 1.0 reduce-window.6
  3.0 0.2 slice_reduce_fusion
  3.2 0.2 reduce-window.9
  3.3 0.7 bitcast_add_fusion.doc
  4.0 1.1 copy.41
  5.2 0.8 copy.45.wq
  6.0 1.1 copy.43
  7.1 0.9 copy.44
  8.0 150.3 %gather.1 = (bf16[2,1024,1024]{2,1,0:T(8,128)(2,1)}, bf16[2,1024,1024]{2,1,0:T(8,128)(2,1)}, s32[2,8,128]{2,1,0:T(8,128)}, f32[2,2,2,8,128]{4,3,2,1,0:T(8,128)},...) custom-call(bf16[1024,1024]{1,0:T(8,128)(2,1)} %refs_9_.1, ...), custom_call_target="tpu_custom_call" | custom-call | tf_op jit(solution)/shard_map/gather/pallas_call | solution.py:358
  158.3 0.8 slice.46
  159.1 0.6 dynamic-slice_bitcast_fusion.fw.refs_5_
  159.7 0.7 eq.53
  160.4 0.1 slice.47
  160.4 0.1 copy.55
  160.5 0.1 compare_convert_fusion.2
  160.6 0.1 reshape.211
  160.7 0.1 concatenate.3
  160.8 0.7 broadcast_in_dim.27.keep
  161.4 0.1 broadcast_bitcast_fusion.1
  161.5 0.1 broadcast_bitcast_fusion
  161.6 0.7 compare_convert_fusion
  162.3 2.0 fusion.1.mask
  164.3 1.3 broadcast_in_dim.11.trail
  165.6 1.4 broadcast_in_dim.10.carr
  167.0 87.7 %attention.1 = (bf16[2048,1024]{1,0:T(8,128)(2,1)}, bf16[2048,512]{1,0:T(8,128)(2,1)}, bf16[2048,1536]{1,0:T(8,128)(2,1)}, bf16[1024,1536]{1,0:T(8,128)(2,1)}, b...) custom-call(bf16[2048,1024]{1,0:T(8,128)(2,1)} %bitcast.98, bf16[2048,1024]{1,0:T(8,128)(2,1)} %bitcast.94, ...), custom_call_target="tpu_custom_call" | custom-call | tf_op jit(solution)/shard_map/attention/pallas_call | solution.py:536
  254.6 73.4 %mlp.1 = (bf16[2048,1024]{1,0:T(8,128)(2,1)}, bf16[1024,2048]{1,0:T(8,128)(2,1)}, bf16[2048,1024]{1,0:T(8,128)(2,1)}, bf16[2048,1024]{1,0:T(8,128)(2,1)}) custom-call(bf16[2048,1024]{1,0:T(8,128)(2,1)} %get-tuple-element.44.mlp_in, bf16[2048,1024]{1,0:T(8,128)(2,1)} %bitcast.95, bf16[2048,512]{1,0:T(8,128)(2,1)} %get-tuple-element.45.o, ...), custom_call_target="tpu_custom_call" | custom-call | tf_op jit(solution)/shard_map/mlp/pallas_call | solution.py:582
  328.1 142.8 %settle.1 = (bf16[2,128,384]{2,1,0:T(8,128)(2,1)}, bf16[128,256]{1,0:T(8,128)(2,1)}, bf16[2,128,512]{2,1,0:T(8,128)(2,1)}, bf16[512,256]{1,0:T(8,128)(2,1)}, f32...) custom-call(bf16[2,2,256,1536]{3,2,1,0:T(8,128)(2,1)} %bitcast.107, ...), custom_call_target="tpu_custom_call" | custom-call | tf_op jit(solution)/shard_map/settle/pallas_call | solution.py:740
  470.9 0.0 copy-start.2
  470.9 0.0 copy-start.1
  470.9 0.8 constant_dynamic-slice_fusion
  471.7 0.5 slice_bitcast_fusion
  472.2 1.5 convert_element_type.68
  473.8 1.1 copy.48
  474.8 0.9 copy.52
  475.8 1.0 convert_bitcast_fusion
  476.8 0.2 copy.50
  477.0 1.0 copy.53
  478.0 0.0 copy-done.2
  478.0 0.0 copy-start
  478.0 0.8 convert_element_type.73
  478.8 0.0 copy-done.1
  478.8 1.3 copy.66
  480.1 1.0 copy-done
  481.1 2.0 copy.67
  (8 shorter events, 0.1 us)
Async XLA Ops:
  470.9 7.1 %copy-start.2 = (bf16[512,256]{1,0:T(8,128)(2,1)S(1)}, bf16[512,256]{1,0:T(8,128)(2,1)}, u32[]{:S(2)}) copy-start(bf16[512,256]{1,0:T(8,128)(2,1)} %get-tuple-element.59) | copy-start | bytes 786436
  470.9 7.9 %copy-start.1 = (bf16[1024,1024]{1,0:T(8,128)(2,1)S(1)}, bf16[1024,1024]{1,0:T(8,128)(2,1)}, u32[]{:S(2)}) copy-start(bf16[1024,1024]{1,0:T(8,128)(2,1)} %get-tuple-element.101) | copy-start | bytes 6291460
  478.0 3.1 copy-start
